TPU v7x, 32 devices: a whole 2x2x4 slice. The times are simulated.
32 devices in a mesh: gather: 8 (over z, core), tm: 4 (over y, x).
Axes of the slice: x: 2, y: 2, z: 4, core: 2. Of those that a mesh axis runs over, the one named last changes fastest.
Arguments:
- records: bfloat16 [8, 4, 80, 512], P('gather', None, None, 'tm'), may hold values from -6 to 6
- lift_weight: bfloat16 [32, 4], replicated, may hold values from -3 to 3
- lift_bias: float32 [32], replicated, may hold values from -2.5 to 2.5
- conv_weight: bfloat16 [4, 32, 32, 3, 3], replicated, may hold values from -0.375 to 0.375
- conv_bias: float32 [4, 32], replicated, may hold values from -1.5 to 1.5
- out_weight: bfloat16 [4, 32], replicated, may hold values from -1 to 1
- live_count: int32 [8], replicated, may hold values from 40 to 80, as said below
- trace_node: int32 [8, 80], replicated, may hold values from 0 to 79, as said below
- node_owner: int32 [80], replicated, may hold values from 0 to 7, as said below
Outputs:
- deblended: float32 [8, 4, 80, 512], P(None, None, 'gather', 'tm')
Inputs may be any that keep to these rules, and one draw needn't show every extreme that they name: `live_count`: some shot gather has all 80 traces live. `trace_node`: each row holds every node once; its first live_count slots hold consecutive nodes in rising order, and the others continue from there cyclically. `node_owner`: every index of gather owns 10 or 9 nodes, and some owns 10.
All inputs are finite; a program needn't handle non-finite values.
Results may differ from a plain program's by a relative error of at most 0.0039.
Values may be sent and summed in bfloat16 or wider, within the bound.
No kernel may reach another device: no remote copies, remote signals or barrier semaphores. Data moves between devices by JAX's collectives and lax.ppermute only.
A program may use at most 64 MiB of HBM per device.

v0:
```python
import functools
import itertools

import jax
import jax.numpy as jnp
from jax import lax
from jax.experimental import pallas as pl
from jax.experimental.pallas import tpu as pltpu
from jax.sharding import PartitionSpec as P

F32 = jnp.float32
BF16 = jnp.bfloat16
CH = 32
CORES = 2
COMPS = 4
GROUP = 8
LANES = GROUP * CH
HALO = 16
QUAD = 4
HALF = QUAD * CH
KROWS = 128
LIFTED = ((0, 0), (0, 1), (1, 1), (1, 0), (0, 2), (1, 2))
PARTS = QUAD * COMPS + 2 * QUAD


def iota(shape, dim):
    return lax.broadcasted_iota(jnp.int32, shape, dim)


def dot(a, b):
    return jnp.dot(a, b, preferred_element_type=F32)


def dot_t(a, b):
    return lax.dot_general(a, b, (((1,), (1,)), ((), ())), preferred_element_type=F32)


def onehot(cond):
    return cond.astype(F32).astype(BF16)


def band_links(dilation, offset):
    return [
        a
        for a in range(3)
        if any(s + GROUP * offset == t + (a - 1) * dilation for s in range(GROUP) for t in range(GROUP))
    ]


def split3(value):
    terms = []
    for _ in range(3):
        term = value.astype(BF16)
        terms.append(term)
        value = value - term.astype(F32)
    return terms


def shot_of(place_ref, n, shots):
    planes = shots // CORES
    plane = place_ref[0] // CORES
    core = place_ref[0] - CORES * plane
    return CORES * (plane ^ (n % planes)) + (core if n < planes else 1 - core)


def couple_of(place_ref, relative):
    return (place_ref[0] // (2 * CORES)) ^ relative


def table_kernel(dils, slots, place_ref, live_ref, trace_ref, owner_ref, pick_ref, keep_ref):
    shots, rows, nodes = pick_ref.shape
    split = round_up(6 * slots, 16)
    me = place_ref[0]

    mine = (owner_ref[...] == me).astype(F32)
    before = onehot(iota((nodes, nodes), 0) < iota((nodes, nodes), 1))
    rank = dot(jnp.broadcast_to(mine, (8, nodes)).astype(BF16), before)[0:1, :]
    node_ids = iota((1, nodes), 1).astype(F32)

    def nodes_of(slot_index):
        held = jnp.where((rank == slot_index.astype(F32)) & (mine > 0.5), 1.0, 0.0)
        node = jnp.sum(held * node_ids, axis=1, keepdims=True)
        there = jnp.sum(held, axis=1, keepdims=True)
        return jnp.where(there > 0.5, node, -1.0e6).astype(jnp.int32)

    row_id = iota((rows, nodes), 0)
    late = row_id >= split
    row_id = jnp.where(late, row_id - split, row_id)
    tap = jnp.zeros((rows, nodes), jnp.int32)
    for m in range(1, 7):
        tap = tap + (row_id >= m * slots).astype(jnp.int32)
    second = (tap >= 3).astype(jnp.int32)
    shift = dils[0] * (tap - 3 * second - 1) + jnp.where(late, 0, dils[1] * (2 * second - 1))
    target = nodes_of(row_id - slots * tap)
    target = jnp.where(tap >= jnp.where(late, 3, 6), -1000000, target + shift)

    node_lane = iota((rows, nodes), 1)
    for n in range(shots):
        s = shot_of(place_ref, n, shots)
        pick_ref[n] = onehot((node_lane == target - trace_ref[s, 0]) & (node_lane < live_ref[s]))

    slot_rows = keep_ref.shape[2]
    own_node = nodes_of(iota((slot_rows, nodes), 0))
    shot_lane = iota((slot_rows, HALF), 1) >> 5
    for c in range(shots // QUAD):
        base = QUAD * couple_of(place_ref, c)
        for b in range(3):
            first = jnp.zeros((slot_rows, HALF), jnp.int32)
            count = jnp.zeros((slot_rows, HALF), jnp.int32)
            for w in range(QUAD):
                at = shot_lane == (w if b == 1 else w ^ 2)
                first = jnp.where(at, trace_ref[base + w, 0], first)
                count = jnp.where(at, live_ref[base + w], count)
            trace = own_node + dils[1] * (b - 1) - first
            keep_ref[c, b] = ((trace >= 0) & (trace < count)).astype(F32)


def started(sources, places, sems):
    copies = [pltpu.make_async_copy(a, b, sems.at[n]) for n, (a, b) in enumerate(zip(sources, places))]
    for copy in copies:
        copy.start()
    return copies


def prep_kernel(dils, slots, place_ref, *refs):
    w0_ref, w1_ref, w2_ref, wide_bias_ref, shift_ref, pick_ref, keep_ref = refs[9:16]
    half = refs[2].shape[0] // 2
    passed = started((refs[7], refs[2].at[half : 2 * half], refs[8]), refs[16:19], refs[27])
    live_ref, trace_ref, cw_ref, lift_ref, lift_bias_ref, bias_ref, owner_ref = refs[19:26]
    sources = (*refs[:2], refs[2].at[0:half], *refs[3:7])
    for copy in started(sources, refs[19:26], refs[26]):
        copy.wait()
    table_kernel(dils, slots, place_ref, live_ref, trace_ref, owner_ref, pick_ref, keep_ref)

    rows8 = [lift_ref[...].astype(F32)] + [term.astype(F32) for term in split3(lift_bias_ref[...])]
    table = jnp.concatenate(rows8 + [jnp.zeros((1, CH), F32)], axis=0).astype(BF16)
    data_rows = 3 * QUAD * COMPS
    r8 = iota((KROWS, 8), 0)
    part = jnp.where(r8 < data_rows, r8 & (COMPS - 1), COMPS + ((r8 >> 2) & 3))
    values = dot(onehot((part == iota((KROWS, 8), 1)) & (r8 < 2 * data_rows)), table).astype(BF16)
    wide = iota((CH, 3 * HALF), 1)
    spread = onehot(iota((CH, 3 * HALF), 0) == (wide & 31))
    rr = iota((KROWS, 3 * HALF), 0)
    cc = iota((KROWS, 3 * HALF), 1)
    row_node = jnp.where(rr < data_rows, rr >> 4, (rr - data_rows) >> 4)
    row_shot = jnp.where(rr < data_rows, rr >> 2, rr) & (QUAD - 1)
    node = sum(jnp.where((cc >> 6) == y, LIFTED[y][1], 0) for y in range(6))
    pair = sum(jnp.where((cc >> 6) == y, LIFTED[y][0], 0) for y in range(6))
    same = (row_node == node) & (row_shot == 2 * pair + ((cc >> 5) & 1)) & (rr < 2 * data_rows)
    w0_ref[...] = jnp.where(same, dot(values, spread), 0.0).astype(BF16)

    widen = onehot((iota((LANES, CH), 0) & 31) == iota((LANES, CH), 1))
    kr = iota((LANES, LANES), 0)
    kc = iota((LANES, LANES), 1)
    same_shot = ((kr >> 5) & 1) == ((kc >> 5) & 1)
    sr = iota((3 * CH, LANES), 0)
    sc = iota((3 * CH, LANES), 1)
    for layer, ref in ((0, w1_ref), (1, w2_ref)):
        base = 3 * layer
        tall = [
            dot_t(widen, cw_ref[(base + a) * 3 * CH : (base + a + 1) * 3 * CH, :]).astype(BF16)
            for a in range(3)
        ]
        for odd, (k_taps, n_taps) in enumerate((((0, 1, 2, 3), (0, 1, 3, 2)), ((1, 0, 3, 2), (1, 0, 2, 3)))):
            place = sum(jnp.where((sc >> 6) == y, n_taps[y], 0) for y in range(4))
            spread2 = onehot(((sr >> 5) == place) & ((sr & 31) == (sc & 31)))
            total = jnp.zeros((LANES, LANES), F32)
            for x in range(4):
                if k_taps[x] < 3:
                    total = jnp.where(((kr >> 6) == x) & same_shot, dot(tall[k_taps[x]], spread2), total)
            ref[odd] = total.astype(BF16)

    span = shift_ref.shape[0]
    window = span - 2 * HALO
    source = iota(shift_ref.shape, 0)
    source = jnp.where(source < window + HALO, source, source + window // 2 - HALO)
    shift_ref[...] = onehot(iota(shift_ref.shape, 1) == source)

    tile = onehot(iota((CH, LANES), 0) == (iota((CH, LANES), 1) & 31))
    wide_bias_ref[...] = sum(dot(term, tile) for term in split3(bias_ref[...]))
    for copy in passed:
        copy.wait()


def band_kernel(dils, blocks, place_ref, *refs):
    cw_ref, out_w_ref, b3_ref, b4_ref, ow_ref = refs
    widen = onehot((iota((LANES, CH), 0) & 31) == iota((LANES, CH), 1))

    er = iota((3 * CH, 3 * LANES), 0)
    ec = iota((3 * CH, 3 * LANES), 1)
    spread3 = onehot(((er >> 5) == (ec >> 8)) & ((er & 31) == (ec & 31)))
    row_lane = iota((LANES, 3 * LANES), 0)
    col_lane = iota((LANES, 3 * LANES), 1) & (LANES - 1)

    def shots_in(lane, block):
        couple = jnp.where(lane < HALF, couple_of(place_ref, 2 * block), couple_of(place_ref, 2 * block + 1))
        return QUAD * couple + ((lane >> 5) & (QUAD - 1))

    def expanded(layer, a):
        base = ((layer - 2) * 3 + a) * 3 * CH
        return dot(dot_t(widen, cw_ref[base : base + 3 * CH, :]).astype(BF16), spread3)

    for layer, ref in ((2, b3_ref), (3, b4_ref)):
        linked_taps = band_links(dils[layer], 0) if blocks == 1 else range(3)
        for out_block in range(blocks):
            for in_block in range(blocks):
                total = jnp.zeros((LANES, 3 * LANES), F32)
                for a in linked_taps:
                    reach = shots_in(col_lane, out_block) + (a - 1) * dils[layer]
                    total = total + jnp.where(shots_in(row_lane, in_block) == reach, expanded(layer, a), 0.0)
                for e in range(3):
                    ref[out_block * blocks + in_block, e * LANES : (e + 1) * LANES, :] = total[
                        :, e * LANES : (e + 1) * LANES
                    ].astype(BF16)

    rows = GROUP * COMPS
    pick = onehot((iota((rows, COMPS), 0) & (COMPS - 1)) == iota((rows, COMPS), 1))
    mine = dot(pick, out_w_ref[...]).astype(BF16)
    tile = onehot(iota((CH, LANES), 0) == (iota((CH, LANES), 1) & 31))
    same = (iota((rows, LANES), 0) >> 2) == (iota((rows, LANES), 1) >> 5)
    ow_ref[...] = jnp.where(same, dot(mine, tile), 0.0).astype(BF16)


def round_up(value, unit):
    return -(-value // unit) * unit


def shifted(value, dilation):
    span = value.shape[0]
    return jnp.concatenate(
        [
            pltpu.roll(value, dilation, axis=0).astype(BF16),
            value.astype(BF16),
            pltpu.roll(value, span - dilation, axis=0).astype(BF16),
        ],
        axis=1,
    )


class Shots:
    def __init__(
        self, dils, windows, step, couple, place_ref, recs, pick_ref, keep_ref, w0_ref, w1_ref, w2_ref,
        bias_ref, shift_ref, part_ref, x2_ref, rec_out_ref,
    ):
        self.dils, self.step, self.couple = dils, step, couple
        self.keep_ref, self.w0_ref, self.w1_ref, self.w2_ref = keep_ref, w0_ref, w1_ref, w2_ref
        self.bias_ref, self.shift_ref, self.x2_ref = bias_ref, shift_ref, x2_ref
        shots, rows, nodes = pick_ref.shape
        planes = shots // CORES
        self.slots = slots = x2_ref.shape[0]
        self.window = window = part_ref.shape[-1]
        self.rows, self.split = part_ref.shape[2], round_up(6 * slots, 16)
        self.span = window + 2 * HALO
        at = place_ref[1]
        self.right_ok = (at < windows - 1).astype(F32)
        self.left_ok = (at > 0).astype(F32)
        self.low_half = iota((self.span, HALF), 1) < CH * CORES

        lane = iota((nodes, 2 * window), 1)
        all_ok = jnp.where(
            lane < window, 1.0, jnp.where(lane < window + window // 2, self.right_ok, self.left_ok)
        ).astype(BF16)

        def put(part, swapped, value):
            for half in range(2):
                lanes = value[:, half * window : (half + 1) * window]
                part_ref[half, part, 0 : self.split] = lanes[0 : self.split]
                part_ref[half, swapped, self.split : rows] = lanes[self.split : rows]

        for x, rec_ref in enumerate(recs):
            n = 2 * couple + x % 2 + (planes if x >= 2 else 0)
            within = shot_of(place_ref, n, shots) & (QUAD - 1)
            edge = rec_ref[COMPS].astype(F32)
            for k in range(COMPS):
                turned = edge if k == 0 else pltpu.roll(edge, window - HALO * k, axis=1)
                both = jnp.concatenate([rec_ref[k], turned.astype(BF16)], axis=1)
                put(within * COMPS + k, (within ^ 2) * COMPS + k, dot(pick_ref[n], both))
            alive = dot(pick_ref[n], all_ok)
            for copy in range(2):
                first = QUAD * COMPS + QUAD * copy
                put(first + within, first + (within ^ 2), alive)

        self.half_rows = part_ref.shape[1] * self.rows
        self.part2 = part_ref.reshape(2 * self.half_rows, window)
        for q in range(slots):
            first = self.split + slots + q
            for half in range(2):
                pair = self.part2[pl.ds(first + (1 - half) * 8 * self.rows, 8, stride=self.rows), :]
                rec_out_ref[q, half * 8 : (half + 1) * 8] = pair

    def inside(self, value):
        w = self.window
        return jnp.concatenate(
            [value[0:w], value[w : w + HALO] * self.right_ok, value[w + HALO :] * self.left_ok], axis=0
        )

    def item_rows(self, q, b):
        start = (3 * (b // 2) * self.slots if b != 1 else self.split) + q
        halves = []
        for half in range(2):
            base = half * self.half_rows + start
            flags = base + QUAD * COMPS * self.rows
            pieces = [
                self.part2[pl.ds(base + a * self.slots, QUAD * COMPS, stride=self.rows), :] for a in range(3)
            ]
            for a in range(3):
                alive = self.part2[pl.ds(flags + a * self.slots, 2 * QUAD, stride=self.rows), :]
                pieces += [alive, alive]
            pieces.append(jnp.zeros((KROWS - 6 * QUAD * COMPS, self.window), F32))
            halves.append(jnp.concatenate(pieces, axis=0).astype(BF16))
        return jnp.concatenate(halves, axis=1)

    def items(self, group):
        return [(group * self.step + i, b) for i in range(self.step) for b in range(3)]

    def first_inputs(self, group):
        items = self.items(group)
        lhs = []
        for n in range(0, len(items), 2):
            some = jnp.concatenate([self.item_rows(q, b) for q, b in items[n : n + 2]], axis=0)
            moved = dot_t(self.shift_ref[...], some).astype(BF16)
            lhs += [moved[:, m : m + KROWS] for m in range(0, moved.shape[1], KROWS)]
        lifted = dot(jnp.concatenate(lhs, axis=0), self.w0_ref[...]).astype(BF16)
        own, other, shared = (lifted[:, m * HALF : (m + 1) * HALF] for m in range(3))
        return jnp.concatenate([own, shared], axis=1), jnp.concatenate([other, shared], axis=1)

    def taps_added(self, even, odd, dilation):
        mid = jnp.where(self.low_half, odd[:, 0:HALF], even[:, 0:HALF])
        late = jnp.where(self.low_half, odd[:, HALF:], even[:, HALF:])
        early = pltpu.roll(jnp.where(self.low_half, even[:, 0:HALF], odd[:, 0:HALF]), HALF // 2, axis=1)
        return (
            pltpu.roll(early, dilation, axis=0) + mid + pltpu.roll(late, self.span - dilation, axis=0)
        )

    def first_layer(self, group, even, odd):
        y_even, y_odd = dot(even, self.w1_ref[0]), dot(odd, self.w1_ref[1])
        x1 = []
        for n, (q, b) in enumerate(self.items(group)):
            at = slice(n * self.span, (n + 1) * self.span)
            old = jnp.where(self.low_half, odd[at, 0:HALF].astype(F32), even[at, 0:HALF].astype(F32))
            total = self.taps_added(y_even[at], y_odd[at], self.dils[0])
            new = jnp.maximum(total + self.bias_ref[0:1, 0:HALF], 0.0)
            x1.append(self.inside((old + new) * self.keep_ref[self.couple, b, q : q + 1, :]))
        even, odd, own = [], [], []
        for i in range(self.step):
            t0, t1, t2 = x1[3 * i : 3 * i + 3]
            t2 = t2.astype(BF16)
            even.append(jnp.concatenate([jnp.where(self.low_half, t0, t1).astype(BF16), t2], axis=1))
            odd.append(jnp.concatenate([jnp.where(self.low_half, t1, t0).astype(BF16), t2], axis=1))
            own.append(t1.astype(BF16))
        return jnp.concatenate(even, axis=0), jnp.concatenate(odd, axis=0), own

    def second_layer(self, group, even, odd, own):
        even, odd = dot(even, self.w2_ref[0]), dot(odd, self.w2_ref[1])
        for i in range(self.step):
            q = group * self.step + i
            at = slice(i * self.span, (i + 1) * self.span)
            total = self.taps_added(even[at], odd[at], self.dils[1])
            new = jnp.maximum(total + self.bias_ref[1:2, 0:HALF], 0.0)
            x2 = (own[i].astype(F32) + new) * self.keep_ref[self.couple, 1, q : q + 1, :]
            self.x2_ref[q] = shifted(self.inside(x2), self.dils[2])


def staged(work):
    inputs, middle = {}, {}
    for t in range(len(work) + 2):
        if 0 <= t - 2:
            stage, group = work[t - 2]
            stage.second_layer(group, *middle.pop(t - 2))
        if 0 <= t - 1 < len(work):
            stage, group = work[t - 1]
            middle[t - 1] = stage.first_layer(group, *inputs.pop(t - 1))
        if t < len(work):
            stage, group = work[t]
            inputs[t] = stage.first_inputs(group)
        yield t


def near_kernel(dils, windows, step, place_ref, *refs):
    pick_ref, keep_ref, w0_ref, w1_ref, w2_ref, bias_ref, shift_ref = refs[:7]
    recs = [refs[7], refs[8], refs[9].at[0], refs[9].at[1]]
    x2_ref, rec_out_ref, part_ref = refs[10:]
    stage = Shots(
        dils, windows, step, 0, place_ref, recs, pick_ref, keep_ref, w0_ref, w1_ref, w2_ref,
        bias_ref, shift_ref, part_ref, x2_ref, rec_out_ref,
    )
    for _ in staged([(stage, group) for group in range(x2_ref.shape[0] // step)]):
        pass


def main_kernel(dils, windows, step, near, place_ref, *refs):
    shots = refs[0].shape[0]
    couples = shots // QUAD
    pick_ref, keep_ref, w0_ref, w1_ref, w2_ref, b3_ref, b4_ref, ow_ref, bias_ref, shift_ref = refs[:10]
    refs = refs[10:]
    rec_refs, refs = refs[: QUAD * (couples - near)], refs[QUAD * (couples - near) :]
    done_refs, refs = refs[: 2 * near], refs[2 * near :]
    out_ref, part_ref, x2_all, rec_all, x3_ref = refs
    blocks = couples // 2
    slots, window = out_ref.shape[1], out_ref.shape[3]
    span = window + 2 * HALO
    right_ok = (place_ref[1] < windows - 1).astype(F32)
    left_ok = (place_ref[1] > 0).astype(F32)

    stages = []
    x2_refs, rec_refs_out = list(done_refs[0::2]), list(done_refs[1::2])
    for c in range(near, couples):
        x2_refs.append(x2_all.at[c - near])
        rec_refs_out.append(rec_all.at[c - near])
        stages.append(
            Shots(
                dils, windows, step, c, place_ref, rec_refs[QUAD * (c - near) : QUAD * (c - near + 1)],
                pick_ref, keep_ref, w0_ref, w1_ref, w2_ref, bias_ref, shift_ref, part_ref.at[c - near],
                x2_refs[-1], rec_refs_out[-1],
            )
        )

    def receiver_layer(parts_of, weights, layer, block, group, out_rows):
        y = None
        for other in range(blocks):
            term = dot(jnp.concatenate(parts_of(other), axis=0), weights[block * blocks + other])
            y = term if y is None else y + term
        results = []
        for i, part in enumerate(parts_of(block)):
            q = group * step + i
            keep = jnp.concatenate([keep_ref[2 * block + c, 1, q : q + 1, :] for c in range(2)], axis=1)
            old = part[:, LANES : 2 * LANES].astype(F32)
            new = jnp.maximum(y[i * out_rows : (i + 1) * out_rows] + bias_ref[layer : layer + 1, :], 0.0)
            results.append((old + new) * keep)
        return results

    def third_layer(group):
        def parts_of(block):
            return [
                jnp.concatenate(
                    [
                        x2_refs[2 * block + c][group * step + i, :, e * HALF : (e + 1) * HALF]
                        for e in range(3)
                        for c in range(2)
                    ],
                    axis=1,
                )
                for i in range(step)
            ]

        for block in range(blocks):
            for i, value in enumerate(receiver_layer(parts_of, b3_ref, 2, block, group, span)):
                value = jnp.concatenate(
                    [
                        value[0:window],
                        value[window : window + HALO] * right_ok,
                        value[window + HALO :] * left_ok,
                    ],
                    axis=0,
                )
                x3_ref[block, group * step + i] = shifted(value, dils[3])[0:window]

    def last_layer(group):
        def parts_of(block):
            return [x3_ref[block, group * step + i] for i in range(step)]

        for block in range(blocks):
            for i, value in enumerate(receiver_layer(parts_of, b4_ref, 3, block, group, window)):
                q = group * step + i
                noise = dot_t(ow_ref[...], value.astype(BF16))
                record = jnp.concatenate([rec_refs_out[2 * block + c][q] for c in range(2)], axis=0)
                done = (record + noise).reshape(GROUP, COMPS, window)
                for c in range(2):
                    first = QUAD * couple_of(place_ref, 2 * block + c)
                    out_ref[pl.ds(first, QUAD), q] = done[c * QUAD : (c + 1) * QUAD]

    groups = slots // step
    work = [(stage, group) for group in range(groups) for stage in stages]
    lag = len(stages)
    for t in itertools.chain(staged(work), range(len(work) + 2, len(work) + 2 + 2 * lag)):
        done, rest = divmod(t - 2, lag)
        if rest == 0 and 0 <= done - 1 < groups:
            third_layer(done - 1)
        if rest == 0 and 0 <= done - 2 < groups:
            last_layer(done - 2)


def divisor(value, limit):
    return max(d for d in range(1, limit + 1) if value % d == 0)


def body(
    records,
    lift_weight,
    lift_bias,
    conv_weight,
    conv_bias,
    out_weight,
    live_count,
    trace_node,
    node_owner,
):
    _, comps, nodes, window = records.shape
    holders = lax.axis_size("gather")
    windows = lax.axis_size("tm")
    shots = holders * records.shape[0]
    couples = shots // QUAD
    blocks = couples // 2
    slots = (nodes + holders - 1) // holders
    dils = (1, 4, 2, 8)
    rows = round_up(6 * slots, 16) + round_up(3 * slots, 16)
    span = window + 2 * HALO

    planes = holders // CORES
    vmem = pl.BlockSpec(memory_space=pltpu.VMEM)
    smem = pl.BlockSpec(memory_space=pltpu.SMEM)
    like = jax.ShapeDtypeStruct

    def after(value, other):
        return lax.optimization_barrier((value, other))[0]

    def kernel(function, operands, specs, outs, scratch, limit, flops, name):
        return pl.pallas_call(
            function,
            out_shape=outs,
            in_specs=[smem] + specs,
            out_specs=jax.tree.map(lambda _: vmem, outs),
            scratch_shapes=scratch,
            compiler_params=pltpu.CompilerParams(vmem_limit_bytes=limit << 20),
            cost_estimate=pl.CostEstimate(flops=flops, bytes_accessed=1 << 10, transcendentals=0),
            name=name,
        )(place, *operands)

    place = jnp.stack([lax.axis_index("gather"), lax.axis_index("tm")]).astype(jnp.int32)
    taps = jnp.transpose(conv_weight, (0, 3, 4, 1, 2)).reshape(-1, CH)

    own = records[0]
    even = lax.axis_index("tm") % 2 == 0
    pack = lambda part: jnp.transpose(part, (1, 0, 2)).reshape(nodes, comps * HALO)
    first, last = pack(own[:, :, :HALO]), pack(own[:, :, window - HALO :])
    got = []
    for begin in range(2):
        pairs = [(w, w + 1) for w in range(begin, windows - 1, 2)]
        pairs += [(b, a) for a, b in pairs]
        got.append(lax.ppermute(jnp.where(even == (begin == 0), last, first), "tm", pairs))
    small = [live_count, trace_node, taps, jnp.transpose(lift_weight), lift_bias[None, :], conv_bias]
    raw = small + [node_owner[None, :], own, out_weight]
    raw = [pltpu.with_memory_space_constraint(a, pltpu.HBM) for a in raw]
    half = (taps.shape[0] // 2, CH)
    scratch = [pltpu.SMEM(a.shape, a.dtype) for a in raw[:2]] + [pltpu.VMEM(half, BF16)]
    scratch += [pltpu.VMEM(a.shape, a.dtype) for a in raw[3:7]]
    w0, w1, w2, wide_bias, shift, pick, keep, own, late_taps, out_taps = kernel(
        functools.partial(prep_kernel, dils, slots),
        raw,
        [pl.BlockSpec(memory_space=pltpu.HBM)] * len(raw),
        (
            like((KROWS, 3 * HALF), BF16),
            like((2, LANES, LANES), BF16),
            like((2, LANES, LANES), BF16),
            like((conv_bias.shape[0], LANES), F32),
            like((span, 2 * window), BF16),
            like((shots, rows, nodes), BF16),
            like((couples, 3, 16, HALF), F32),
            like(own.shape, BF16),
            like(half, BF16),
            like(out_weight.shape, BF16),
        ),
        scratch + [pltpu.SemaphoreType.DMA((7,)), pltpu.SemaphoreType.DMA((3,))],
        16,
        10**5,
        "weights",
    )
    right, left = jnp.where(even, got[0], got[1]), jnp.where(even, got[1], got[0])
    sent = jnp.concatenate([own, jnp.concatenate([right, left], axis=1)[None]], axis=0)


    def exchanged(block, distance):
        return lax.ppermute(block, "gather", [(g, g ^ distance) for g in range(holders)])

    near_blocks = [sent, exchanged(sent, CORES)]
    far = [exchanged(sent, CORES * r) for r in range(2, planes)]
    near_blocks.append(exchanged(jnp.stack(near_blocks), 1))

    b3, b4, ow = kernel(
        functools.partial(band_kernel, dils, blocks),
        [late_taps, out_taps],
        [vmem] * 2,
        (
            like((blocks * blocks, 3 * LANES, LANES), BF16),
            like((blocks * blocks, 3 * LANES, LANES), BF16),
            like((GROUP * COMPS, LANES), BF16),
        ),
        [],
        16,
        10**10,
        "bands",
    )

    step = divisor(slots, 5)
    row_stride = round_up(rows, 16) + 8
    x2 = like((slots, span, 3 * HALF), BF16)
    held = like((slots, QUAD * COMPS, window), F32)
    parts = (2, PARTS + 1, row_stride, window)
    operands = [after(pick, ow), keep, w0, w1, w2, wide_bias, shift, *near_blocks]
    near = kernel(
        functools.partial(near_kernel, dils, windows, step),
        operands,
        [vmem] * len(operands),
        (x2, held),
        [pltpu.VMEM(parts, F32)],
        24,
        10**5,
        "near",
    )

    operands = [pick, keep, w0, w1, w2, b3, b4, ow, wide_bias, shift]
    for r in range(0, len(far), 2):
        operands += far[r : r + 2] + [exchanged(after(block, near[1]), 1) for block in far[r : r + 2]]
    operands += near
    out = kernel(
        functools.partial(main_kernel, dils, windows, step, 1),
        operands,
        [vmem] * len(operands),
        like((shots, slots, comps, window), F32),
        [
            pltpu.VMEM((couples - 1, *parts), F32),
            pltpu.VMEM((couples - 1, *x2.shape), BF16),
            pltpu.VMEM((couples - 1, *held.shape), F32),
            pltpu.VMEM((blocks, slots, window, 3 * LANES), BF16),
        ],
        36,
        4 * 10**9,
        "layers",
    )
    return jnp.transpose(out, (0, 2, 1, 3))


def solution(mesh):
    return jax.shard_map(
        body,
        mesh=mesh,
        in_specs=(P("gather", None, None, "tm"), P(), P(), P(), P(), P(), P(), P(), P()),
        out_specs=P(None, None, "gather", "tm"),
        check_vma=False,
    )
```

profile of v0, /device:TPU:29, one launch (start us, length us, event | category | flops | bytes accessed | tf_op | source)
XLA Modules:
  0.0 32.5 jit_solution(8309409495667410387)
XLA Ops:
  0.0 1.1 %select_bitcast_fusion.1 = (bf16[80,4,16]{2,0,1:T(8,128)(2,1)S(1)}, bf16[80,4,16]{2,0,1:T(8,128)(2,1)S(1)}) fusion(pred[]{:T(512)S(6)} %eq.8, bf16[4,80,128]{2,1,0:T(8,128)(2,1)} %bitcast.22, pred[]{:T(512)S(6)} %eq.9), kind=kLoop, calls=%fused_computation.3 | loop fusion | flops 10240 | bytes 40962 | tf_op jit(solution)/shard_map/jit(_where)/select_n | solution.py:540
  1.1 0.1 copy.12
  1.1 0.1 copy.13
  1.3 1.3 %collective-permute-start = (bf16[80,64]{1,0:T(8,128)(2,1)S(1)}, bf16[80,64]{1,0:T(8,128)(2,1)S(1)}, u32[]{:S(2)}, u32[]{:S(2)}) collective-permute-start(bf16[80,64]{1,0:T(8,128)(2,1)S(1)} %copy.13), channel_id=1, source_target_pairs={{0,1},{2,3},{1,0},{3,2},{4,5},{6,7},{5,4},{7,6},{8,9},{10,11},{9,8... | collective-permute-start | bytes 30728 | tf_op jit(solution)/shard_map/ppermute | solution.py:540
  2.5 0.1 copy.14
  2.6 0.1 copy.15
  2.7 2.1 %collective-permute-start.1 = (bf16[80,64]{1,0:T(8,128)(2,1)S(1)}, bf16[80,64]{1,0:T(8,128)(2,1)S(1)}, u32[]{:S(2)}, u32[]{:S(2)}) collective-permute-start(bf16[80,64]{1,0:T(8,128)(2,1)S(1)} %copy.15), channel_id=1, source_target_pairs={{1,2},{2,1},{5,6},{6,5},{9,10},{10,9},{13,14},{14,13},{17,18},{18,... | collective-permute-start | bytes 30728 | tf_op jit(solution)/shard_map/ppermute | solution.py:540
  4.8 0.1 pad_add_fusion.place_ref
  4.9 2.7 %weights.1 = (bf16[128,384]{1,0:T(8,128)(2,1)S(1)}, bf16[2,256,256]{2,1,0:T(8,128)(2,1)S(1)}, bf16[2,256,256]{2,1,0:T(8,128)(2,1)S(1)}, f32[4,256]{1,0:T(4,128)S...) custom-call(s32[2]{0:T(128)S(1)} %pad_add_fusion.place_ref, ...), custom_call_target="tpu_custom_call" | custom-call | flops 100000 | bytes 1024 | tf_op jit(solution)/shard_map/weights/pallas_call | solution.py:518
  7.6 0.0 collective-permute-done
  7.6 0.5 %collective-permute-done.1 = bf16[80,64]{1,0:T(8,128)(2,1)S(1)} collective-permute-done((bf16[80,64]{1,0:T(8,128)(2,1)S(1)}, bf16[80,64]{1,0:T(8,128)(2,1)S(1)}, u32[]{:S(2)}, u32[]{:S(2)}) %collective-permute-start.1) | collective-permute-done | bytes 10272 | tf_op jit(solution)/shard_map/ppermute | solution.py:540
  8.2 0.1 maximum_bitcast_fusion
  8.3 0.2 collective-permute-start.4
  8.5 1.1 %collective-permute-start.3 = (bf16[5,80,128]{2,1,0:T(8,128)(2,1)S(1)}, bf16[5,80,128]{2,1,0:T(8,128)(2,1)S(1)}, u32[]{:S(2)}, u32[]{:S(2)}) collective-permute-start(bf16[5,80,128]{2,1,0:T(8,128)(2,1)S(1)} %get-tuple-element.42.refs_7_), channel_id=1, source_target_pairs={{0,24},{4,28},{8,16},{12,20},{16,8},{20,12},{24,0},{28,4},{1,25},{... | collective-permute-start | bytes 307208 | tf_op jit(solution)/shard_map/ppermute | solution.py:573
  9.6 1.4 %collective-permute-start.2 = (bf16[5,80,128]{2,1,0:T(8,128)(2,1)S(1)}, bf16[5,80,128]{2,1,0:T(8,128)(2,1)S(1)}, u32[]{:S(2)}, u32[]{:S(2)}) collective-permute-start(bf16[5,80,128]{2,1,0:T(8,128)(2,1)S(1)} %get-tuple-element.42.refs_7_), channel_id=1, source_target_pairs={{0,16},{4,20},{8,24},{12,28},{16,0},{20,4},{24,8},{28,12},{1,17},{... | collective-permute-start | bytes 307208 | tf_op jit(solution)/shard_map/ppermute | solution.py:573
  11.0 0.9 %collective-permute-done.4.refs_8_ = bf16[5,80,128]{2,1,0:T(8,128)(2,1)S(1)} collective-permute-done((bf16[5,80,128]{2,1,0:T(8,128)(2,1)S(1)}, bf16[5,80,128]{2,1,0:T(8,128)(2,1)S(1)}, u32[]{:S(2)}, u32[]{:S(2)}) %collective-permute-start.4) | collective-permute-done | bytes 102432 | tf_op jit(solution)/shard_map/ppermute | solution.py:573
  11.9 4.8 %collective-permute-start.5 = (bf16[2,5,80,128]{3,2,1,0:T(8,128)(2,1)S(1)}, bf16[2,5,80,128]{3,2,1,0:T(8,128)(2,1)S(1)}, u32[]{:S(2)}, u32[]{:S(2)}) collective-permute-start(bf16[2,5,80,128]{3,2,1,0:T(8,128)(2,1)S(1)} %pad_maximum_fusion), channel_id=1, source_target_pairs={{0,4},{4,0},{8,12},{12,8},{16,20},{20,16},{24,28},{28,24},{1,5},{5... | collective-permute-start | bytes 614408 | tf_op jit(solution)/shard_map/ppermute | solution.py:573
  16.6 1.7 %bands.1 = (bf16[1,768,256]{2,1,0:T(8,128)(2,1)S(1)}, bf16[1,768,256]{2,1,0:T(8,128)(2,1)S(1)}, bf16[32,256]{1,0:T(8,128)(2,1)S(1)}) custom-call(s32[2]{0:T(128)S(1)} %pad_add_fusion.place_ref, bf16[576,32]{1,0:T(8,128)(2,1)S(1)} %get-tuple-element.28.refs_0_, bf16[4,32]{1,0:T(4,128)(2,1)S(1)} %get-tuple-element.29.refs_1_), custom_call_target="tpu_custom_call" | custom-call | flops 10000000000 | bytes 1024 | tf_op jit(solution)/shard_map/bands/pallas_call | solution.py:518
  18.3 5.0 %near.1 = (bf16[10,160,384]{2,1,0:T(8,128)(2,1)S(1)}, f32[10,16,128]{2,1,0:T(8,128)S(1)}) custom-call(s32[2]{0:T(128)S(1)} %pad_add_fusion.place_ref, bf16[8,96,80]{2,1,0:T(8,128)(2,1)S(1)} %get-tuple-element.36.refs_0_, f32[2,3,16,128]{3,2,1,0:T(8,128)S(1)} %get-tuple-element.24.refs_1_, bf16[128,384]{1,0:T(8,128)(2,1)S(1)} %get-tuple-element.25.refs_2_, ...), custom_call_target="tpu_custom_call" | custom-call | flops 100000 | bytes 1024 | tf_op jit(solution)/shard_map/near/pallas_call | solution.py:518
  23.3 0.1 collective-permute-start.7
  23.4 0.5 %collective-permute-start.6 = (bf16[5,80,128]{2,1,0:T(8,128)(2,1)S(1)}, bf16[5,80,128]{2,1,0:T(8,128)(2,1)S(1)}, u32[]{:S(2)}, u32[]{:S(2)}) collective-permute-start(bf16[5,80,128]{2,1,0:T(8,128)(2,1)S(1)} %collective-permute-done.2.refs_10_), channel_id=1, source_target_pairs={{0,4},{4,0},{8,12},{12,8},{16,20},{20,16},{24,28},{28,24},{1,5},{5... | collective-permute-start | bytes 307208 | tf_op jit(solution)/shard_map/ppermute | solution.py:573
  23.9 0.8 %collective-permute-done.7.refs_13_ = bf16[5,80,128]{2,1,0:T(8,128)(2,1)S(1)} collective-permute-done((bf16[5,80,128]{2,1,0:T(8,128)(2,1)S(1)}, bf16[5,80,128]{2,1,0:T(8,128)(2,1)S(1)}, u32[]{:S(2)}, u32[]{:S(2)}) %collective-permute-start.7) | collective-permute-done | bytes 102432 | tf_op jit(solution)/shard_map/ppermute | solution.py:573
  24.7 0.2 collective-permute-done.6.refs_12_
  24.9 7.7 %layers.1 = f32[8,10,4,128]{3,2,1,0:T(4,128)} custom-call(s32[2]{0:T(128)S(1)} %pad_add_fusion.place_ref, bf16[8,96,80]{2,1,0:T(8,128)(2,1)S(1)} %get-tuple-element.36.refs_0_, f32[2,3,16,128]{3,2,1,0:T(8,128)S(1)} %get-tuple-element.24.refs_1_, bf16[128,384]{1,0:T(8,128)(2,1)S(1)} %get-tuple-element.25.refs_2_, ...), custom_call_target="tpu_custom_call" | custom-call | flops 4000000000 | bytes 1024 | tf_op jit(solution)/shard_map/layers/pallas_call | solution.py:518
  (6 shorter events, 0.1 us)
Async XLA Ops:
  1.3 6.4 %collective-permute-start = (bf16[80,64]{1,0:T(8,128)(2,1)S(1)}, bf16[80,64]{1,0:T(8,128)(2,1)S(1)}, u32[]{:S(2)}, u32[]{:S(2)}) collective-permute-start(bf16[80,64]{1,0:T(8,128)(2,1)S(1)} %copy.13), channel_id=1, source_target_pairs={{0,1},{2,3},{1,0},{3,2},{4,5},{6,7},{5,4},{7,6},{8,9},{10,11},{9,8... | collective-permute-start | bytes 30728 | tf_op jit(solution)/shard_map/ppermute | solution.py:540
  2.7 5.4 %collective-permute-start.1 = (bf16[80,64]{1,0:T(8,128)(2,1)S(1)}, bf16[80,64]{1,0:T(8,128)(2,1)S(1)}, u32[]{:S(2)}, u32[]{:S(2)}) collective-permute-start(bf16[80,64]{1,0:T(8,128)(2,1)S(1)} %copy.15), channel_id=1, source_target_pairs={{1,2},{2,1},{5,6},{6,5},{9,10},{10,9},{13,14},{14,13},{17,18},{18,... | collective-permute-start | bytes 30728 | tf_op jit(solution)/shard_map/ppermute | solution.py:540
  8.3 3.6 %collective-permute-start.4 = (bf16[5,80,128]{2,1,0:T(8,128)(2,1)S(1)}, bf16[5,80,128]{2,1,0:T(8,128)(2,1)S(1)}, u32[]{:S(2)}, u32[]{:S(2)}) collective-permute-start(bf16[5,80,128]{2,1,0:T(8,128)(2,1)S(1)} %get-tuple-element.42.refs_7_), channel_id=1, source_target_pairs={{0,8},{4,12},{8,0},{12,4},{16,24},{20,28},{24,16},{28,20},{1,9},{5... | collective-permute-start | bytes 307208 | tf_op jit(solution)/shard_map/ppermute | solution.py:573
  8.5 14.8 %collective-permute-start.3 = (bf16[5,80,128]{2,1,0:T(8,128)(2,1)S(1)}, bf16[5,80,128]{2,1,0:T(8,128)(2,1)S(1)}, u32[]{:S(2)}, u32[]{:S(2)}) collective-permute-start(bf16[5,80,128]{2,1,0:T(8,128)(2,1)S(1)} %get-tuple-element.42.refs_7_), channel_id=1, source_target_pairs={{0,24},{4,28},{8,16},{12,20},{16,8},{20,12},{24,0},{28,4},{1,25},{... | collective-permute-start | bytes 307208 | tf_op jit(solution)/shard_map/ppermute | solution.py:573
  9.6 13.9 %collective-permute-start.2 = (bf16[5,80,128]{2,1,0:T(8,128)(2,1)S(1)}, bf16[5,80,128]{2,1,0:T(8,128)(2,1)S(1)}, u32[]{:S(2)}, u32[]{:S(2)}) collective-permute-start(bf16[5,80,128]{2,1,0:T(8,128)(2,1)S(1)} %get-tuple-element.42.refs_7_), channel_id=1, source_target_pairs={{0,16},{4,20},{8,24},{12,28},{16,0},{20,4},{24,8},{28,12},{1,17},{... | collective-permute-start | bytes 307208 | tf_op jit(solution)/shard_map/ppermute | solution.py:573
  11.9 6.5 %collective-permute-start.5 = (bf16[2,5,80,128]{3,2,1,0:T(8,128)(2,1)S(1)}, bf16[2,5,80,128]{3,2,1,0:T(8,128)(2,1)S(1)}, u32[]{:S(2)}, u32[]{:S(2)}) collective-permute-start(bf16[2,5,80,128]{3,2,1,0:T(8,128)(2,1)S(1)} %pad_maximum_fusion), channel_id=1, source_target_pairs={{0,4},{4,0},{8,12},{12,8},{16,20},{20,16},{24,28},{28,24},{1,5},{5... | collective-permute-start | bytes 614408 | tf_op jit(solution)/shard_map/ppermute | solution.py:573
  23.3 1.4 %collective-permute-start.7 = (bf16[5,80,128]{2,1,0:T(8,128)(2,1)S(1)}, bf16[5,80,128]{2,1,0:T(8,128)(2,1)S(1)}, u32[]{:S(2)}, u32[]{:S(2)}) collective-permute-start(bf16[5,80,128]{2,1,0:T(8,128)(2,1)S(1)} %collective-permute-done.3.refs_11_), channel_id=1, source_target_pairs={{0,4},{4,0},{8,12},{12,8},{16,20},{20,16},{24,28},{28,24},{1,5},{5... | collective-permute-start | bytes 307208 | tf_op jit(solution)/shard_map/ppermute | solution.py:573
  23.4 1.4 %collective-permute-start.6 = (bf16[5,80,128]{2,1,0:T(8,128)(2,1)S(1)}, bf16[5,80,128]{2,1,0:T(8,128)(2,1)S(1)}, u32[]{:S(2)}, u32[]{:S(2)}) collective-permute-start(bf16[5,80,128]{2,1,0:T(8,128)(2,1)S(1)} %collective-permute-done.2.refs_10_), channel_id=1, source_target_pairs={{0,4},{4,0},{8,12},{12,8},{16,20},{20,16},{24,28},{28,24},{1,5},{5... | collective-permute-start | bytes 307208 | tf_op jit(solution)/shard_map/ppermute | solution.py:573
where the time goes:
time: 32.7 us; the launch traced here: 32.5 us
  Pallas kernels  17.1 us (52%)
  starting transfers between devices  11.4 us (35%)
  waiting for transfers between devices  2.32 us (7%)
  other arithmetic  1.26 us (4%)
  local copies, waits for them, and re-layouts  0.37 us (1%)
    pallas_call x4, Pallas kernels, kernel(): pl.pallas_call(function, out_shape=outs, in_specs=[smem] + specs, out_spe...  17.1 us
    ppermute x6, starting transfers between devices, exchanged(): lax.ppermute(block, 'gather', [(g, g ^ distance) for g in range(holders)])  8.05 us
    ppermute x2, starting transfers between devices, body(): lax.ppermute(jnp.where(even == (begin == 0), last, first), 'tm', pairs)  3.38 us
    ppermute x6, waiting for transfers between devices, exchanged(): lax.ppermute(block, 'gather', [(g, g ^ distance) for g in range(holders)])  1.82 us
    select_n x1, other arithmetic, body(): jnp.where(even == (begin == 0), last, first)  1.05 us
  transfers between devices with their start and end apart: 8, of which 4 were waited for; matrix products, arithmetic and copies ran while one was open for 1% of the time, Pallas kernels for 29%

commit v1 on v0

--- a/solution.py
+++ b/solution.py
@@ -364,6 +364,7 @@
 def staged(work):
     inputs, middle = {}, {}
     for t in range(len(work) + 2):
+        yield t
         if 0 <= t - 2:
             stage, group = work[t - 2]
             stage.second_layer(group, *middle.pop(t - 2))
@@ -373,7 +374,6 @@
         if t < len(work):
             stage, group = work[t]
             inputs[t] = stage.first_inputs(group)
-        yield t
 
 
 def near_kernel(dils, windows, step, place_ref, *refs):
@@ -474,10 +474,10 @@
     lag = len(stages)
     for t in itertools.chain(staged(work), range(len(work) + 2, len(work) + 2 + 2 * lag)):
         done, rest = divmod(t - 2, lag)
+        if rest == 0 and 0 <= done - 2 < groups:
+            last_layer(done - 2)
         if rest == 0 and 0 <= done - 1 < groups:
             third_layer(done - 1)
-        if rest == 0 and 0 <= done - 2 < groups:
-            last_layer(done - 2)
 
 
 def divisor(value, limit):

time: 32.7 us -> 33 us (level)
  no operation moved by 1% of the time
where the time goes in v1:
time: 33 us; the launch traced here: 32.8 us
  Pallas kernels  17.4 us (53%)
  starting transfers between devices  11.4 us (35%)
  waiting for transfers between devices  2.32 us (7%)
  other arithmetic  1.26 us (4%)
  local copies, waits for them, and re-layouts  0.37 us (1%)
    pallas_call x4, Pallas kernels, kernel(): pl.pallas_call(function, out_shape=outs, in_specs=[smem] + specs, out_spe...  17.4 us
    ppermute x6, starting transfers between devices, exchanged(): lax.ppermute(block, 'gather', [(g, g ^ distance) for g in range(holders)])  8.05 us
    ppermute x2, starting transfers between devices, body(): lax.ppermute(jnp.where(even == (begin == 0), last, first), 'tm', pairs)  3.38 us
    ppermute x6, waiting for transfers between devices, exchanged(): lax.ppermute(block, 'gather', [(g, g ^ distance) for g in range(holders)])  1.82 us
    select_n x1, other arithmetic, body(): jnp.where(even == (begin == 0), last, first)  1.05 us
  transfers between devices with their start and end apart: 8, of which 4 were waited for; matrix products, arithmetic and copies ran while one was open for 1% of the time, Pallas kernels for 29%

profile of v1, /device:TPU:29, one launch (start us, length us, event | category | flops | bytes accessed | tf_op | source)
XLA Modules:
  0.0 32.8 jit_solution(10221144307888078971)
XLA Ops:
  0.0 1.1 %select_bitcast_fusion.1 = (bf16[80,4,16]{2,0,1:T(8,128)(2,1)S(1)}, bf16[80,4,16]{2,0,1:T(8,128)(2,1)S(1)}) fusion(pred[]{:T(512)S(6)} %eq.8, bf16[4,80,128]{2,1,0:T(8,128)(2,1)} %bitcast.22, pred[]{:T(512)S(6)} %eq.9), kind=kLoop, calls=%fused_computation.3 | loop fusion | flops 10240 | bytes 40962 | tf_op jit(solution)/shard_map/jit(_where)/select_n | solution.py:540
  1.1 0.1 copy.12
  1.1 0.1 copy.13
  1.3 1.3 %collective-permute-start = (bf16[80,64]{1,0:T(8,128)(2,1)S(1)}, bf16[80,64]{1,0:T(8,128)(2,1)S(1)}, u32[]{:S(2)}, u32[]{:S(2)}) collective-permute-start(bf16[80,64]{1,0:T(8,128)(2,1)S(1)} %copy.13), channel_id=1, source_target_pairs={{0,1},{2,3},{1,0},{3,2},{4,5},{6,7},{5,4},{7,6},{8,9},{10,11},{9,8... | collective-permute-start | bytes 30728 | tf_op jit(solution)/shard_map/ppermute | solution.py:540
  2.5 0.1 copy.14
  2.6 0.1 copy.15
  2.7 2.1 %collective-permute-start.1 = (bf16[80,64]{1,0:T(8,128)(2,1)S(1)}, bf16[80,64]{1,0:T(8,128)(2,1)S(1)}, u32[]{:S(2)}, u32[]{:S(2)}) collective-permute-start(bf16[80,64]{1,0:T(8,128)(2,1)S(1)} %copy.15), channel_id=1, source_target_pairs={{1,2},{2,1},{5,6},{6,5},{9,10},{10,9},{13,14},{14,13},{17,18},{18,... | collective-permute-start | bytes 30728 | tf_op jit(solution)/shard_map/ppermute | solution.py:540
  4.8 0.1 pad_add_fusion.place_ref
  4.9 2.7 %weights.1 = (bf16[128,384]{1,0:T(8,128)(2,1)S(1)}, bf16[2,256,256]{2,1,0:T(8,128)(2,1)S(1)}, bf16[2,256,256]{2,1,0:T(8,128)(2,1)S(1)}, f32[4,256]{1,0:T(4,128)S...) custom-call(s32[2]{0:T(128)S(1)} %pad_add_fusion.place_ref, ...), custom_call_target="tpu_custom_call" | custom-call | flops 100000 | bytes 1024 | tf_op jit(solution)/shard_map/weights/pallas_call | solution.py:518
  7.6 0.5 %collective-permute-done.1 = bf16[80,64]{1,0:T(8,128)(2,1)S(1)} collective-permute-done((bf16[80,64]{1,0:T(8,128)(2,1)S(1)}, bf16[80,64]{1,0:T(8,128)(2,1)S(1)}, u32[]{:S(2)}, u32[]{:S(2)}) %collective-permute-start.1) | collective-permute-done | bytes 10272 | tf_op jit(solution)/shard_map/ppermute | solution.py:540
  8.2 0.1 maximum_bitcast_fusion
  8.3 0.2 collective-permute-start.4
  8.5 1.1 %collective-permute-start.3 = (bf16[5,80,128]{2,1,0:T(8,128)(2,1)S(1)}, bf16[5,80,128]{2,1,0:T(8,128)(2,1)S(1)}, u32[]{:S(2)}, u32[]{:S(2)}) collective-permute-start(bf16[5,80,128]{2,1,0:T(8,128)(2,1)S(1)} %get-tuple-element.42.refs_7_), channel_id=1, source_target_pairs={{0,24},{4,28},{8,16},{12,20},{16,8},{20,12},{24,0},{28,4},{1,25},{... | collective-permute-start | bytes 307208 | tf_op jit(solution)/shard_map/ppermute | solution.py:573
  9.6 1.4 %collective-permute-start.2 = (bf16[5,80,128]{2,1,0:T(8,128)(2,1)S(1)}, bf16[5,80,128]{2,1,0:T(8,128)(2,1)S(1)}, u32[]{:S(2)}, u32[]{:S(2)}) collective-permute-start(bf16[5,80,128]{2,1,0:T(8,128)(2,1)S(1)} %get-tuple-element.42.refs_7_), channel_id=1, source_target_pairs={{0,16},{4,20},{8,24},{12,28},{16,0},{20,4},{24,8},{28,12},{1,17},{... | collective-permute-start | bytes 307208 | tf_op jit(solution)/shard_map/ppermute | solution.py:573
  11.0 0.9 %collective-permute-done.4.refs_8_ = bf16[5,80,128]{2,1,0:T(8,128)(2,1)S(1)} collective-permute-done((bf16[5,80,128]{2,1,0:T(8,128)(2,1)S(1)}, bf16[5,80,128]{2,1,0:T(8,128)(2,1)S(1)}, u32[]{:S(2)}, u32[]{:S(2)}) %collective-permute-start.4) | collective-permute-done | bytes 102432 | tf_op jit(solution)/shard_map/ppermute | solution.py:573
  11.9 4.8 %collective-permute-start.5 = (bf16[2,5,80,128]{3,2,1,0:T(8,128)(2,1)S(1)}, bf16[2,5,80,128]{3,2,1,0:T(8,128)(2,1)S(1)}, u32[]{:S(2)}, u32[]{:S(2)}) collective-permute-start(bf16[2,5,80,128]{3,2,1,0:T(8,128)(2,1)S(1)} %pad_maximum_fusion), channel_id=1, source_target_pairs={{0,4},{4,0},{8,12},{12,8},{16,20},{20,16},{24,28},{28,24},{1,5},{5... | collective-permute-start | bytes 614408 | tf_op jit(solution)/shard_map/ppermute | solution.py:573
  16.6 1.7 %bands.1 = (bf16[1,768,256]{2,1,0:T(8,128)(2,1)S(1)}, bf16[1,768,256]{2,1,0:T(8,128)(2,1)S(1)}, bf16[32,256]{1,0:T(8,128)(2,1)S(1)}) custom-call(s32[2]{0:T(128)S(1)} %pad_add_fusion.place_ref, bf16[576,32]{1,0:T(8,128)(2,1)S(1)} %get-tuple-element.28.refs_0_, bf16[4,32]{1,0:T(4,128)(2,1)S(1)} %get-tuple-element.29.refs_1_), custom_call_target="tpu_custom_call" | custom-call | flops 10000000000 | bytes 1024 | tf_op jit(solution)/shard_map/bands/pallas_call | solution.py:518
  18.3 0.0 collective-permute-done.5.refs_9_
  18.3 5.0 %near.1 = (bf16[10,160,384]{2,1,0:T(8,128)(2,1)S(1)}, f32[10,16,128]{2,1,0:T(8,128)S(1)}) custom-call(s32[2]{0:T(128)S(1)} %pad_add_fusion.place_ref, bf16[8,96,80]{2,1,0:T(8,128)(2,1)S(1)} %get-tuple-element.36.refs_0_, f32[2,3,16,128]{3,2,1,0:T(8,128)S(1)} %get-tuple-element.24.refs_1_, bf16[128,384]{1,0:T(8,128)(2,1)S(1)} %get-tuple-element.25.refs_2_, ...), custom_call_target="tpu_custom_call" | custom-call | flops 100000 | bytes 1024 | tf_op jit(solution)/shard_map/near/pallas_call | solution.py:518
  23.3 0.1 collective-permute-start.7
  23.4 0.5 %collective-permute-start.6 = (bf16[5,80,128]{2,1,0:T(8,128)(2,1)S(1)}, bf16[5,80,128]{2,1,0:T(8,128)(2,1)S(1)}, u32[]{:S(2)}, u32[]{:S(2)}) collective-permute-start(bf16[5,80,128]{2,1,0:T(8,128)(2,1)S(1)} %collective-permute-done.2.refs_10_), channel_id=1, source_target_pairs={{0,4},{4,0},{8,12},{12,8},{16,20},{20,16},{24,28},{28,24},{1,5},{5... | collective-permute-start | bytes 307208 | tf_op jit(solution)/shard_map/ppermute | solution.py:573
  23.9 0.8 %collective-permute-done.7.refs_13_ = bf16[5,80,128]{2,1,0:T(8,128)(2,1)S(1)} collective-permute-done((bf16[5,80,128]{2,1,0:T(8,128)(2,1)S(1)}, bf16[5,80,128]{2,1,0:T(8,128)(2,1)S(1)}, u32[]{:S(2)}, u32[]{:S(2)}) %collective-permute-start.7) | collective-permute-done | bytes 102432 | tf_op jit(solution)/shard_map/ppermute | solution.py:573
  24.7 0.2 collective-permute-done.6.refs_12_
  24.9 8.0 %layers.1 = f32[8,10,4,128]{3,2,1,0:T(4,128)} custom-call(s32[2]{0:T(128)S(1)} %pad_add_fusion.place_ref, bf16[8,96,80]{2,1,0:T(8,128)(2,1)S(1)} %get-tuple-element.36.refs_0_, f32[2,3,16,128]{3,2,1,0:T(8,128)S(1)} %get-tuple-element.24.refs_1_, bf16[128,384]{1,0:T(8,128)(2,1)S(1)} %get-tuple-element.25.refs_2_, ...), custom_call_target="tpu_custom_call" | custom-call | flops 4000000000 | bytes 1024 | tf_op jit(solution)/shard_map/layers/pallas_call | solution.py:518
  (6 shorter events, 0.1 us)
Async XLA Ops:
  1.3 6.4 %collective-permute-start = (bf16[80,64]{1,0:T(8,128)(2,1)S(1)}, bf16[80,64]{1,0:T(8,128)(2,1)S(1)}, u32[]{:S(2)}, u32[]{:S(2)}) collective-permute-start(bf16[80,64]{1,0:T(8,128)(2,1)S(1)} %copy.13), channel_id=1, source_target_pairs={{0,1},{2,3},{1,0},{3,2},{4,5},{6,7},{5,4},{7,6},{8,9},{10,11},{9,8... | collective-permute-start | bytes 30728 | tf_op jit(solution)/shard_map/ppermute | solution.py:540
  2.7 5.4 %collective-permute-start.1 = (bf16[80,64]{1,0:T(8,128)(2,1)S(1)}, bf16[80,64]{1,0:T(8,128)(2,1)S(1)}, u32[]{:S(2)}, u32[]{:S(2)}) collective-permute-start(bf16[80,64]{1,0:T(8,128)(2,1)S(1)} %copy.15), channel_id=1, source_target_pairs={{1,2},{2,1},{5,6},{6,5},{9,10},{10,9},{13,14},{14,13},{17,18},{18,... | collective-permute-start | bytes 30728 | tf_op jit(solution)/shard_map/ppermute | solution.py:540
  8.3 3.6 %collective-permute-start.4 = (bf16[5,80,128]{2,1,0:T(8,128)(2,1)S(1)}, bf16[5,80,128]{2,1,0:T(8,128)(2,1)S(1)}, u32[]{:S(2)}, u32[]{:S(2)}) collective-permute-start(bf16[5,80,128]{2,1,0:T(8,128)(2,1)S(1)} %get-tuple-element.42.refs_7_), channel_id=1, source_target_pairs={{0,8},{4,12},{8,0},{12,4},{16,24},{20,28},{24,16},{28,20},{1,9},{5... | collective-permute-start | bytes 307208 | tf_op jit(solution)/shard_map/ppermute | solution.py:573
  8.5 14.8 %collective-permute-start.3 = (bf16[5,80,128]{2,1,0:T(8,128)(2,1)S(1)}, bf16[5,80,128]{2,1,0:T(8,128)(2,1)S(1)}, u32[]{:S(2)}, u32[]{:S(2)}) collective-permute-start(bf16[5,80,128]{2,1,0:T(8,128)(2,1)S(1)} %get-tuple-element.42.refs_7_), channel_id=1, source_target_pairs={{0,24},{4,28},{8,16},{12,20},{16,8},{20,12},{24,0},{28,4},{1,25},{... | collective-permute-start | bytes 307208 | tf_op jit(solution)/shard_map/ppermute | solution.py:573
  9.6 13.9 %collective-permute-start.2 = (bf16[5,80,128]{2,1,0:T(8,128)(2,1)S(1)}, bf16[5,80,128]{2,1,0:T(8,128)(2,1)S(1)}, u32[]{:S(2)}, u32[]{:S(2)}) collective-permute-start(bf16[5,80,128]{2,1,0:T(8,128)(2,1)S(1)} %get-tuple-element.42.refs_7_), channel_id=1, source_target_pairs={{0,16},{4,20},{8,24},{12,28},{16,0},{20,4},{24,8},{28,12},{1,17},{... | collective-permute-start | bytes 307208 | tf_op jit(solution)/shard_map/ppermute | solution.py:573
  11.9 6.5 %collective-permute-start.5 = (bf16[2,5,80,128]{3,2,1,0:T(8,128)(2,1)S(1)}, bf16[2,5,80,128]{3,2,1,0:T(8,128)(2,1)S(1)}, u32[]{:S(2)}, u32[]{:S(2)}) collective-permute-start(bf16[2,5,80,128]{3,2,1,0:T(8,128)(2,1)S(1)} %pad_maximum_fusion), channel_id=1, source_target_pairs={{0,4},{4,0},{8,12},{12,8},{16,20},{20,16},{24,28},{28,24},{1,5},{5... | collective-permute-start | bytes 614408 | tf_op jit(solution)/shard_map/ppermute | solution.py:573
  23.3 1.4 %collective-permute-start.7 = (bf16[5,80,128]{2,1,0:T(8,128)(2,1)S(1)}, bf16[5,80,128]{2,1,0:T(8,128)(2,1)S(1)}, u32[]{:S(2)}, u32[]{:S(2)}) collective-permute-start(bf16[5,80,128]{2,1,0:T(8,128)(2,1)S(1)} %collective-permute-done.3.refs_11_), channel_id=1, source_target_pairs={{0,4},{4,0},{8,12},{12,8},{16,20},{20,16},{24,28},{28,24},{1,5},{5... | collective-permute-start | bytes 307208 | tf_op jit(solution)/shard_map/ppermute | solution.py:573
  23.4 1.4 %collective-permute-start.6 = (bf16[5,80,128]{2,1,0:T(8,128)(2,1)S(1)}, bf16[5,80,128]{2,1,0:T(8,128)(2,1)S(1)}, u32[]{:S(2)}, u32[]{:S(2)}) collective-permute-start(bf16[5,80,128]{2,1,0:T(8,128)(2,1)S(1)} %collective-permute-done.2.refs_10_), channel_id=1, source_target_pairs={{0,4},{4,0},{8,12},{12,8},{16,20},{20,16},{24,28},{28,24},{1,5},{5... | collective-permute-start | bytes 307208 | tf_op jit(solution)/shard_map/ppermute | solution.py:573
